TPU v7x, 32 devices: a whole 2x2x4 slice. The times are simulated.
32 devices in a mesh: groups: 2 (over y), virt: 4 (over z), occ: 2 (over x), rep: 2 (over core).
Axes of the slice: x: 2, y: 2, z: 4, core: 2. Of those that a mesh axis runs over, the one named last changes fastest.
Arguments:
- amplitudes: bfloat16 [4096, 1024], P(('groups', 'occ'), 'virt'), parts along dimension 0, may hold values from -6 to 6
- live_mask: int32 [128, 8], P(('groups', 'occ'), 'virt'), parts along dimension 0, may hold values 0 or 1
- integrals: bfloat16 [16, 4, 128, 128], P(('groups', 'virt'), 'rep'), parts along dimension 0, may hold values from -0.25 to 0.25
- coupled_tiles: int32 [16, 4], P(('groups', 'virt'), 'rep'), parts along dimension 0, may hold values from 0 to 7, all different within a row
Outputs:
- residual: bfloat16 [4096, 1024], P(('groups', 'occ'), ('virt', 'rep')), parts along dimension 0
There are 2 independent parts, one for each index of `groups`. A program takes and returns all parts, laid end to end along the dimension named above; each array names one. Nothing has to cross between parts.
Inputs may be any that keep to these rules, and one draw needn't show every extreme that they name: `coupled_tiles`: each row names 4 different tiles.
All inputs are finite; a program needn't handle non-finite values. No bound on the sum of `live_mask` on one device may be relied on, other than what follows from the above.
Results may differ from a plain program's by a relative error of at most 0.001.
Values may be sent and summed in bfloat16 or wider, within the bound.
A program may use at most 128 MiB of HBM per device.

v0:
```python
import jax
import jax.numpy as jnp
from jax import lax
from jax.sharding import PartitionSpec as P


def per_device(amplitudes, live_mask, integrals, coupled_tiles):
    tile_width = integrals.shape[2]
    virt_count = lax.axis_size("virt")
    rep_count = lax.axis_size("rep")
    arrived, live_tiles = (
        lax.all_to_all(amplitudes, "virt", split_axis=0, concat_axis=1, tiled=True),
        lax.all_to_all(live_mask, "virt", split_axis=0, concat_axis=1, tiled=True),
    )
    row_count = arrived.shape[0]
    tile_count = live_tiles.shape[1]
    block_rows = row_count // live_tiles.shape[0]
    masked = arrived.reshape(live_tiles.shape[0], block_rows, tile_count, tile_width)
    masked = masked * live_tiles[:, None, :, None].astype(arrived.dtype)
    masked = masked.reshape(row_count, tile_count, tile_width)
    col_width = tile_count * tile_width // (virt_count * rep_count)
    panel_blocks, panel_index = (integrals, coupled_tiles)
    blocks = lax.all_gather(panel_blocks, "virt", axis=0, tiled=True)
    tile_index = lax.all_gather(panel_index, "virt", axis=0, tiled=True)
    count, coupled = tile_index.shape
    picked = jnp.take(masked, tile_index.reshape(-1), axis=1)
    picked = picked.reshape(row_count, count, coupled * tile_width)
    weights = blocks.reshape(count, coupled * tile_width, tile_width)
    contrib = jnp.einsum("rnx,nxa->rna", picked, weights, preferred_element_type=jnp.float32)
    shares = lax.psum_scatter(
        contrib.reshape(row_count, virt_count, rep_count, col_width),
        "rep",
        scatter_dimension=2,
        tiled=True,
    )
    rounded = shares.reshape(row_count, virt_count, col_width).astype(jnp.bfloat16)
    returned = lax.all_to_all(rounded, "virt", split_axis=1, concat_axis=0, tiled=True)
    return returned.reshape(row_count * virt_count, col_width)


def solution(mesh):
    return jax.shard_map(
        per_device,
        mesh=mesh,
        in_specs=(
            P(("groups", "occ"), "virt"),
            P(("groups", "occ"), "virt"),
            P(("groups", "virt"), "rep", None, None),
            P(("groups", "virt"), "rep"),
        ),
        out_specs=P(("groups", "occ"), ("virt", "rep")),
        check_vma=False,
    )
```

profile of v0, /device:TPU:0, one launch (start us, length us, event | category | flops | bytes accessed | tf_op | source)
XLA Modules:
  0.0 70.6 jit_solution(9812203532049615973)
XLA Ops:
  0.0 0.8 %all_to_all.36 = s32[4,8,2]{1,0,2:T(4,128)S(1)} reshape(s32[32,2]{0,1:T(2,128)} %param.5) | data formatting | bytes 512 | tf_op jit(solution)/shard_map/all_to_all | solution.py:13
  0.8 0.6 copy.21
  1.4 6.3 %all-to-all-start.1 = ((s32[4,8,2]{1,2,0:T(2,128)}), s32[4,8,2]{1,2,0:T(2,128)S(1)}, u32[]{:S(2)}, u32[]{:S(2)}) async-start(s32[4,8,2]{1,2,0:T(2,128)} %copy.21), calls=%async_computation.1 | async-start | bytes 8192 | tf_op jit(solution)/shard_map/all_to_all | solution.py:13
  7.7 0.0 copy-start.1
  7.7 0.7 copy-done.1
  8.4 11.4 %all-gather = s32[4,2,2]{2,1,0:T(2,128)S(1)} all-gather(s32[1,2,2]{2,1,0:T(2,128)S(1)} %bitcast.52), channel_id=1, replica_groups=mesh['groups'=2,'virt'=4,'occ'=2,'rep'=2] {'virt'}, dimensions={0}, use_global_device_ids=true | all-gather | bytes 80 | tf_op jit(solution)/shard_map/all_gather | solution.py:24
  19.7 0.1 reshape.77
  19.8 0.0 all-to-all-done.1
  19.8 0.0 copy-start
  19.8 3.6 %all-to-all-start = ((bf16[4,256,256]{2,1,0:T(8,128)(2,1)}), bf16[4,256,256]{2,1,0:T(8,128)(2,1)S(1)}, u32[]{:S(2)}, u32[]{:S(2)}) async-start(bf16[4,256,256]{2,1,0:T(8,128)(2,1)} %bitcast.49), calls=%async_computation | async-start | bytes 1048576 | tf_op jit(solution)/shard_map/all_to_all | solution.py:12
  23.5 0.1 copy.26
  23.6 0.0 copy-start.2
  23.6 0.7 copy-done.2
  24.2 0.6 dynamic-slice
  24.8 0.0 copy-done
  24.8 21.7 %all_gather.7 = bf16[8,2,128,128]{3,2,1,0:T(8,128)(2,1)S(1)} all-gather(bf16[2,2,128,128]{3,2,1,0:T(8,128)(2,1)S(1)} %copy-done), channel_id=1, replica_groups=mesh['groups'=2,'virt'=4,'occ'=2,'rep'=2] {'virt'}, dimensions={0}, use_global_device_ids=true | all-gather | bytes 655360 | tf_op jit(solution)/shard_map/all_gather | solution.py:23
  46.5 0.1 broadcast_bitcast_fusion
  46.6 0.1 mul.13
  46.7 0.1 mul.14
  46.8 0.0 all-to-all-done
  46.8 0.2 copy.20
  47.0 0.3 copy.22
  47.3 0.3 broadcast_multiply_fusion
  47.6 0.7 %gather_fusion = bf16[16,256,128]{2,1,0:T(8,128)(2,1)S(1)} fusion(bf16[256,8,128]{2,0,1:T(8,128)(2,1)S(1)} %broadcast_multiply_fusion, s32[1024]{0:T(1024)S(1)} %pad_clamp_fusion), kind=kCustom, calls=%fused_computation | custom fusion | bytes 2097216 | tf_op jit(solution)/shard_map/jit(_take)/gather | solution.py:26
  48.4 0.5 copy.23
  48.9 0.4 bitcast_select_fusion
  49.4 0.5 fusion.2
  49.9 6.3 %all-reduce.2 = bf16[256,4,2,128]{3,0,2,1:T(8,128)(2,1)S(1)} all-reduce(f32[256,4,2,128]{3,0,2,1:T(8,128)S(1)} %bitcast.44), channel_id=2, replica_groups=mesh['groups'=2,'virt'=4,'occ'=2,'rep'=2] {'rep'}, use_global_device_ids=true, to_apply=%region_0.1.clone | all-reduce | flops 262144 | bytes 1572864
  56.1 0.7 fusion
  56.8 13.1 %all_to_all.44 = bf16[256,4,128]{2,0,1:T(8,128)(2,1)S(1)} all-to-all(bf16[256,4,128]{2,0,1:T(8,128)(2,1)S(1)} %fusion), channel_id=1, replica_groups=mesh['groups'=2,'virt'=4,'occ'=2,'rep'=2] {'virt'}, dimensions={1} | all-to-all | bytes 524288 | tf_op jit(solution)/shard_map/all_to_all | solution.py:37
  69.9 0.7 copy.32
  (4 shorter events, 0.0 us)
Async XLA Ops:
  1.4 18.5 %all-to-all-start.1 = ((s32[4,8,2]{1,2,0:T(2,128)}), s32[4,8,2]{1,2,0:T(2,128)S(1)}, u32[]{:S(2)}, u32[]{:S(2)}) async-start(s32[4,8,2]{1,2,0:T(2,128)} %copy.21), calls=%async_computation.1 | async-start | bytes 8192 | tf_op jit(solution)/shard_map/all_to_all | solution.py:13
  7.7 0.7 copy-start.1
  19.8 5.0 %copy-start = (bf16[2,2,128,128]{3,2,1,0:T(8,128)(2,1)S(1)}, bf16[2,2,128,128]{3,2,1,0:T(8,128)(2,1)}, u32[]{:S(2)}) copy-start(bf16[2,2,128,128]{3,2,1,0:T(8,128)(2,1)} %param.6) | copy-start | bytes 393220
  19.8 26.9 %all-to-all-start = ((bf16[4,256,256]{2,1,0:T(8,128)(2,1)}), bf16[4,256,256]{2,1,0:T(8,128)(2,1)S(1)}, u32[]{:S(2)}, u32[]{:S(2)}) async-start(bf16[4,256,256]{2,1,0:T(8,128)(2,1)} %bitcast.49), calls=%async_computation | async-start | bytes 1048576 | tf_op jit(solution)/shard_map/all_to_all | solution.py:12
  23.6 0.7 copy-start.2
where the time goes:
time: 70.9 us; the launch traced here: 70.6 us
  blocking collectives  52.4 us (74%)
  starting transfers between devices  9.93 us (14%)
  local copies, waits for them, and re-layouts  6.83 us (10%)
  other arithmetic  0.81 us (1%)
    all_gather x1, blocking collectives, per_device(): blocks = lax.all_gather(panel_blocks, 'virt', axis=0, tiled=True)  21.7 us
    all_to_all x1, blocking collectives, per_device(): lax.all_to_all(rounded, 'virt', split_axis=1, concat_axis=0, tiled=True)  13.1 us
    all_gather x1, blocking collectives, per_device(): tile_index = lax.all_gather(panel_index, 'virt', axis=0, tiled=True)  11.4 us
    all_to_all x1, starting transfers between devices, per_device(): lax.all_to_all(live_mask, 'virt', split_axis=0, concat_axis=1, tiled=True)  6.32 us
    unnamed x1, blocking collectives  6.27 us
    all_to_all x1, starting transfers between devices, per_device(): lax.all_to_all(amplitudes, 'virt', split_axis=0, concat_axis=1, tiled=True)  3.62 us
    unnamed x9, local copies, waits for them, and re-layouts  2.71 us
  transfers between devices with their start and end apart: 2, of which 0 were waited for; matrix products, arithmetic and copies ran while one was open for 1% of the time, Pallas kernels for 0%

commit v1 on v0

v1 whole, which is shorter than its diff:
```python
import functools

import jax
import jax.numpy as jnp
from jax import lax
from jax.experimental import pallas as pl
from jax.experimental.pallas import tpu as pltpu
from jax.sharding import PartitionSpec as P

MESH = pl.DeviceIdType.MESH
CHUNKS = 4


def ladder_kernel(
    amps, live, ints, pattern, out,
    held, panels, codes, codes_s, dense, staged,
    load_sem, send_r, send_l, recv_sem,
    pan_load, pan_recv, pan_send, code_load, code_recv, code_send, code_copy,
    own_sem, mate_sem, back_sem, out_recv,
):
    count = lax.axis_size("virt")
    cores = lax.axis_size("rep")
    z = lax.axis_index("virt")
    r = lax.axis_index("rep")
    mate = 1 - r
    last = count - 1
    tiles, ks, width, _ = ints.shape
    half = held.shape[1]
    rows = half // CHUNKS
    block = amps.shape[0] // live.shape[0]
    is_end = jnp.logical_or(z == 0, z == last)
    works = jnp.logical_not(is_end)
    helps = jnp.logical_or(z == 1, z == last - 1)
    helper = jnp.where(z == 0, 1, last - 1)
    helped = jnp.where(z == 1, 0, last)

    barrier = pltpu.get_barrier_semaphore()
    pl.semaphore_signal(barrier, inc=1, device_id={"rep": mate}, device_id_type=MESH)

    @pl.when(z > 0)
    def _():
        for c in range(cores):
            pl.semaphore_signal(barrier, inc=1, device_id={"virt": z - 1, "rep": c}, device_id_type=MESH)

    @pl.when(z < last)
    def _():
        for c in range(cores):
            pl.semaphore_signal(barrier, inc=1, device_id={"virt": z + 1, "rep": c}, device_id_type=MESH)

    def part(c):
        return pl.ds(pl.multiple_of(c * rows, rows), rows)

    def load(c):
        start = pl.multiple_of(r * half + c * rows, rows)
        return pltpu.make_async_copy(amps.at[pl.ds(start, rows)], held.at[z, part(c)], load_sem.at[c])

    for c in range(CHUNKS):
        load(c).start()
    pan_in = pltpu.make_async_copy(ints, panels.at[0, r], pan_load)
    code_in = pltpu.make_async_copy(pattern, codes.at[0, r], code_load)
    pan_in.start()
    code_in.start()

    def remote(src, dst, send, recv, **where):
        return pltpu.make_async_remote_copy(
            src_ref=src, dst_ref=dst, send_sem=send, recv_sem=recv, device_id=where, device_id_type=MESH
        )

    pan_mate = remote(panels.at[0, r], panels.at[0, r], pan_send.at[0], pan_recv.at[0], rep=mate)
    code_mate = remote(codes.at[0, r], codes.at[0, r], code_send.at[0], code_recv.at[0], rep=mate)
    pan_help = remote(panels.at[0, r], panels.at[1, r], pan_send.at[1], pan_recv.at[1], virt=helper)
    code_help = remote(codes.at[0, r], codes.at[1, r], code_send.at[1], code_recv.at[1], virt=helper)
    pan_pass = remote(panels.at[1, r], panels.at[1, r], pan_send.at[2], pan_recv.at[2], rep=mate)
    code_pass = remote(codes.at[1, r], codes.at[1, r], code_send.at[2], code_recv.at[2], rep=mate)

    def to_right(j, c):
        return remote(held.at[j, part(c)], held.at[j, part(c)], send_r.at[j, c], recv_sem.at[j, c], virt=z + 1)

    def to_left(j, c):
        return remote(held.at[j, part(c)], held.at[j, part(c)], send_l.at[j, c], recv_sem.at[j, c], virt=z - 1)

    goes_right = z + 1 <= last - 1
    goes_left = z - 1 >= 1

    pl.semaphore_wait(barrier, 1 + cores * ((z > 0).astype(jnp.int32) + (z < last).astype(jnp.int32)))

    pan_in.wait()
    code_in.wait()

    @pl.when(is_end)
    def _():
        pan_help.start()
        code_help.start()

    def mask(c):
        def one(b, _):
            at = pl.multiple_of(c * rows + b * block, block)
            which = (r * half + c * rows) // block + b
            for t in range(tiles):
                keep = live[which, t].astype(jnp.float32)
                keep = jnp.full((block, width), keep, jnp.float32).astype(held.dtype)
                view = held.at[z, pl.ds(at, block), pl.ds(t * width, width)]
                view[...] = view[...] * keep
            return 0

        lax.fori_loop(0, rows // block, one, 0, unroll=rows // block <= 8)

    for c in range(CHUNKS):
        load(c).wait()
        mask(c)

        @pl.when(goes_right)
        def _():
            to_right(z, c).start()

        @pl.when(goes_left)
        def _():
            to_left(z, c).start()

        if c == 0:
            @pl.when(works)
            def _():
                pan_mate.start()
                code_mate.start()

    def build(g):
        copy = pltpu.make_async_copy(codes.at[g], codes_s.at[g], code_copy)
        copy.start()
        copy.wait()

        def one(j, _):
            for t in range(tiles):
                for i in range(tiles):
                    total = jnp.zeros((width, width), dense.dtype)
                    for c in range(cores):
                        for k in range(ks):
                            hit = (codes_s[g, c, i, k] == j * tiles + t).astype(jnp.float32)
                            hit = jnp.full((width, width), hit, jnp.float32).astype(dense.dtype)
                            total = total + hit * panels[g, c, i, k]
                    dense[g, j, pl.ds(t * width, width), pl.ds(i * width, width)] = total
            return 0

        lax.fori_loop(0, count, one, 0)

    def arrive(j, c):
        to_right(j, c).wait_recv()

    def forward(c):
        def one(d, _):
            left, right = z - d, z + d

            @pl.when(jnp.logical_and(left >= 0, goes_right))
            def _():
                arrive(left, c)
                to_right(left, c).start()

            @pl.when(jnp.logical_and(right <= last, goes_left))
            def _():
                arrive(right, c)
                to_left(right, c).start()

            return 0

        lax.fori_loop(1, count, one, 0)

    def settle(c):
        def one(d, _):
            left, right = z - d, z + d

            @pl.when(jnp.logical_and(left >= 0, jnp.logical_not(goes_right)))
            def _():
                arrive(left, c)

            @pl.when(jnp.logical_and(right <= last, jnp.logical_not(goes_left)))
            def _():
                arrive(right, c)

            return 0

        lax.fori_loop(1, count, one, 0)

    def spot(owner, c):
        return pl.ds(pl.multiple_of(owner * half + c * rows, rows), rows)

    def own_out(c):
        return pltpu.make_async_copy(staged.at[0, r, part(c)], out.at[spot(r, c)], own_sem.at[c])

    def mate_out(c):
        return remote(
            staged.at[0, mate, part(c)], out.at[spot(r, c)], mate_sem.at[c], out_recv.at[r, c], rep=mate
        )

    def back_out(core, c):
        return remote(
            staged.at[1, core, part(c)], out.at[spot(r, c)], back_sem.at[core, c], out_recv.at[r, c],
            virt=helped, rep=core,
        )

    step = min(rows, 128)

    def multiply(g, c):
        def one(s, _):
            at = pl.ds(pl.multiple_of(c * rows + s * step, step), step)
            total = jnp.zeros((step, tiles * width), jnp.float32)
            for j in range(count):
                total = total + jnp.dot(held[j, at], dense[g, j], preferred_element_type=jnp.float32)
            for i in range(tiles):
                staged[g, i, at] = total[:, i * width : (i + 1) * width].astype(staged.dtype)
            return 0

        lax.fori_loop(0, rows // step, one, 0)

    @pl.when(works)
    def _():
        pan_mate.wait_recv()
        code_mate.wait_recv()
        build(0)

    @pl.when(helps)
    def _():
        pan_help.wait_recv()
        code_help.wait_recv()
        pan_pass.start()
        code_pass.start()

    @pl.when(works)
    def _():
        forward(0)

    @pl.when(helps)
    def _():
        pan_pass.wait_recv()
        code_pass.wait_recv()
        build(1)

    @pl.when(works)
    def _():
        for c in range(CHUNKS):
            if c + 1 < CHUNKS:
                forward(c + 1)
            settle(c)

            @pl.when(helps)
            def _():
                multiply(1, c)
                for core in range(cores):
                    back_out(core, c).start()

            multiply(0, c)
            mate_out(c).start()
            own_out(c).start()

    @pl.when(is_end)
    def _():
        pan_help.wait_send()
        code_help.wait_send()
        for c in range(CHUNKS):
            for core in range(cores):
                remote(
                    staged.at[0, 0, part(c)], out.at[spot(core, c)], mate_sem.at[c], out_recv.at[core, c], rep=mate
                ).wait_recv()

    for c in range(CHUNKS):
        @pl.when(goes_right)
        def _():
            to_right(z, c).wait_send()

        @pl.when(goes_left)
        def _():
            to_left(z, c).wait_send()

    @pl.when(works)
    def _():
        pan_mate.wait_send()
        code_mate.wait_send()
        for c in range(CHUNKS):
            def one(d, _):
                left, right = z - d, z + d

                @pl.when(jnp.logical_and(left >= 0, goes_right))
                def _():
                    to_right(left, c).wait_send()

                @pl.when(jnp.logical_and(right <= last, goes_left))
                def _():
                    to_left(right, c).wait_send()

                return 0

            lax.fori_loop(1, count, one, 0)
            own_out(c).wait()
            mate_out(c).wait_send()
            remote(
                staged.at[0, 0, part(c)], out.at[spot(mate, c)], mate_sem.at[c], out_recv.at[mate, c], rep=mate
            ).wait_recv()

    @pl.when(helps)
    def _():
        pan_pass.wait_send()
        code_pass.wait_send()
        for c in range(CHUNKS):
            for core in range(cores):
                back_out(core, c).wait_send()


def per_device(amplitudes, live_mask, integrals, coupled_tiles):
    count = lax.axis_size("virt")
    cores = lax.axis_size("rep")
    tiles, ks, width, _ = integrals.shape
    half = amplitudes.shape[0] // cores
    dma = pltpu.SemaphoreType.DMA
    kind = amplitudes.dtype
    return pl.pallas_call(
        ladder_kernel,
        out_shape=jax.ShapeDtypeStruct((amplitudes.shape[0], width), kind),
        in_specs=[
            pl.BlockSpec(memory_space=pl.ANY),
            pl.BlockSpec(memory_space=pltpu.SMEM),
            pl.BlockSpec(memory_space=pl.ANY),
            pl.BlockSpec(memory_space=pl.ANY),
        ],
        out_specs=pl.BlockSpec(memory_space=pl.ANY),
        scratch_shapes=[
            pltpu.VMEM((count, half, tiles * width), kind),
            pltpu.VMEM((2, cores, tiles, ks, width, width), kind),
            pltpu.VMEM((2, cores, tiles, ks), jnp.int32),
            pltpu.SMEM((2, cores, tiles, ks), jnp.int32),
            pltpu.VMEM((2, count, tiles * width, tiles * width), kind),
            pltpu.VMEM((2, tiles, half, width), kind),
            dma((CHUNKS,)),
            dma((count, CHUNKS)),
            dma((count, CHUNKS)),
            dma((count, CHUNKS)),
            dma(()),
            dma((3,)),
            dma((3,)),
            dma(()),
            dma((3,)),
            dma((3,)),
            dma(()),
            dma((CHUNKS,)),
            dma((CHUNKS,)),
            dma((cores, CHUNKS)),
            dma((cores, CHUNKS)),
        ],
        compiler_params=pltpu.CompilerParams(
            collective_id=0, has_side_effects=True, vmem_limit_bytes=48 * 1024 * 1024
        ),
    )(amplitudes, live_mask, integrals, coupled_tiles)


def solution(mesh):
    return jax.shard_map(
        per_device,
        mesh=mesh,
        in_specs=(
            P(("groups", "occ"), "virt"),
            P(("groups", "occ"), "virt"),
            P(("groups", "virt"), "rep", None, None),
            P(("groups", "virt"), "rep"),
        ),
        out_specs=P(("groups", "occ"), ("virt", "rep")),
        check_vma=False,
    )
```

time: 70.9 us -> 26.7 us (0.38)
  blocking collectives: 52.4 us -> 0 us
  Pallas kernels: 0 us -> 23.1 us
  starting transfers between devices: 9.93 us -> 0 us
  local copies, waits for them, and re-layouts: 6.83 us -> 3.43 us
  other arithmetic: 0.81 us -> 0 us
    all_gather x2 -> x0, blocking collectives: 33.1 us -> none  [the longest x1 21.7 us: per_device(): blocks = lax.all_gather(panel_blocks, 'virt', axis=0, tiled=True)]
    pallas_call x0 -> x1, Pallas kernels: none -> 23.1 us  [per_device(): pl.pallas_call(ladder_kernel, out_shape=jax.ShapeDtypeStruct((amplitudes....]
    all_to_all x1 -> x0, blocking collectives: 13.1 us -> none  [per_device(): lax.all_to_all(rounded, 'virt', split_axis=1, concat_axis=0, tiled=True)]
    all_to_all x2 -> x0, starting transfers between devices: 9.93 us -> none  [the longest x1 6.32 us: per_device(): lax.all_to_all(live_mask, 'virt', split_axis=0, concat_axis=1, tiled=True)]
    unnamed x1 -> x0, blocking collectives: 6.27 us -> none
    all_to_all x3 -> x0, local copies, waits for them, and re-layouts: 1.57 us -> none  [the longest x2 1.36 us: per_device(): lax.all_to_all(live_mask, 'virt', split_axis=0, concat_axis=1, tiled=True)]
    gather x2 -> x0, local copies, waits for them, and re-layouts: 1.28 us -> none  [per_device(): picked = jnp.take(masked, tile_index.reshape(-1), axis=1)]
    unnamed x9 -> x8, local copies, waits for them, and re-layouts: 2.71 us -> 3.43 us
  transfers between devices with their start and end apart: 2 -> 0, of which waited for: 0 -> 0; matrix products, arithmetic and copies ran while one was open for 1% -> 0% of each run, Pallas kernels for 0% -> 0%
where the time goes in v1:
time: 26.7 us; the launch traced here: 26.6 us
  Pallas kernels  23.1 us (87%)
  local copies, waits for them, and re-layouts  3.43 us (13%)
    pallas_call x1, Pallas kernels, per_device(): pl.pallas_call(ladder_kernel, out_shape=jax.ShapeDtypeStruct((amplitudes....  23.1 us
    unnamed x8, local copies, waits for them, and re-layouts  3.43 us

profile of v1, /device:TPU:0, one launch (start us, length us, event | category | flops | bytes accessed | tf_op | source)
XLA Modules:
  0.0 26.6 jit_solution(6550062994340172880)
XLA Ops:
  0.0 0.0 copy-start.2
  0.0 0.8 %copy.5.live = s32[32,2]{1,0:T(8,128)S(1)} copy(s32[32,2]{0,1:T(2,128)} %param.5) | data formatting | bytes 512 | tf_op args[1]
  0.8 0.0 copy-done.2
  0.8 0.0 copy-start
  0.8 1.0 %copy-done = bf16[1024,256]{1,0:T(8,128)(2,1)S(1)} copy-done((bf16[1024,256]{1,0:T(8,128)(2,1)S(1)}, bf16[1024,256]{1,0:T(8,128)(2,1)}, u32[]{:S(2)}) %copy-start) | copy-done | bytes 524312
  1.8 0.0 copy-start.1
  1.8 0.9 %copy-done.1 = bf16[2,2,128,128]{3,2,1,0:T(8,128)(2,1)S(1)} copy-done((bf16[2,2,128,128]{3,2,1,0:T(8,128)(2,1)S(1)}, bf16[2,2,128,128]{3,2,1,0:T(8,128)(2,1)}, u32[]{:S(2)}) %copy-start.1) | copy-done | bytes 131096
  2.7 23.1 %shard_map.46 = bf16[1024,128]{1,0:T(8,128)(2,1)S(1)} custom-call(bf16[1024,256]{1,0:T(8,128)(2,1)S(1)} %copy-done, s32[32,2]{1,0:T(8,128)S(1)} %copy.5.live, bf16[2,2,128,128]{3,2,1,0:T(8,128)(2,1)S(1)} %copy-done.1, s32[2,2]{1,0:T(2,128)S(1)} %copy-done.2), custom_call_target="tpu_custom_call" | custom-call | tf_op jit(solution)/shard_map/pallas_call | solution.py:313
  25.8 0.7 %copy.7 = bf16[1024,128]{1,0:T(8,128)(2,1)} copy(bf16[1024,128]{1,0:T(8,128)(2,1)S(1)} %shard_map.46) | data formatting | bytes 524288
Async XLA Ops:
  0.0 0.8 %copy-start.2 = (s32[2,2]{1,0:T(2,128)S(1)}, s32[2,2]{1,0:T(2,128)}, u32[]{:S(2)}) copy-start(s32[2,2]{1,0:T(2,128)} %pattern.1) | copy-start | bytes 52
  0.8 1.0 %copy-start = (bf16[1024,256]{1,0:T(8,128)(2,1)S(1)}, bf16[1024,256]{1,0:T(8,128)(2,1)}, u32[]{:S(2)}) copy-start(bf16[1024,256]{1,0:T(8,128)(2,1)} %amps.1) | copy-start | bytes 1572868
  1.8 0.9 %copy-start.1 = (bf16[2,2,128,128]{3,2,1,0:T(8,128)(2,1)S(1)}, bf16[2,2,128,128]{3,2,1,0:T(8,128)(2,1)}, u32[]{:S(2)}) copy-start(bf16[2,2,128,128]{3,2,1,0:T(8,128)(2,1)} %ints.1) | copy-start | bytes 393220

commit v2 on v1

--- a/solution.py
+++ b/solution.py
@@ -12,9 +12,9 @@
 
 
 def ladder_kernel(
-    amps, live, ints, pattern, out,
-    held, panels, codes, codes_s, dense, staged,
-    load_sem, send_r, send_l, recv_sem,
+    amps, live_in, ints, pattern, out,
+    live, held, panels, codes, codes_s, dense, staged,
+    live_sem, load_sem, send_r, send_l, recv_sem,
     pan_load, pan_recv, pan_send, code_load, code_recv, code_send, code_copy,
     own_sem, mate_sem, back_sem, out_recv,
 ):
@@ -27,7 +27,7 @@
     tiles, ks, width, _ = ints.shape
     half = held.shape[1]
     rows = half // CHUNKS
-    block = amps.shape[0] // live.shape[0]
+    block = amps.shape[0] // live.shape[1]
     is_end = jnp.logical_or(z == 0, z == last)
     works = jnp.logical_not(is_end)
     helps = jnp.logical_or(z == 1, z == last - 1)
@@ -54,8 +54,9 @@
         start = pl.multiple_of(r * half + c * rows, rows)
         return pltpu.make_async_copy(amps.at[pl.ds(start, rows)], held.at[z, part(c)], load_sem.at[c])
 
-    for c in range(CHUNKS):
-        load(c).start()
+    live_load = pltpu.make_async_copy(live_in, live, live_sem)
+    live_load.start()
+    lax.fori_loop(0, CHUNKS, lambda c, _: (load(c).start(), 0)[1], 0)
     pan_in = pltpu.make_async_copy(ints, panels.at[0, r], pan_load)
     code_in = pltpu.make_async_copy(pattern, codes.at[0, r], code_load)
     pan_in.start()
@@ -82,22 +83,13 @@
     goes_right = z + 1 <= last - 1
     goes_left = z - 1 >= 1
 
-    pl.semaphore_wait(barrier, 1 + cores * ((z > 0).astype(jnp.int32) + (z < last).astype(jnp.int32)))
-
-    pan_in.wait()
-    code_in.wait()
-
-    @pl.when(is_end)
-    def _():
-        pan_help.start()
-        code_help.start()
 
     def mask(c):
         def one(b, _):
             at = pl.multiple_of(c * rows + b * block, block)
             which = (r * half + c * rows) // block + b
             for t in range(tiles):
-                keep = live[which, t].astype(jnp.float32)
+                keep = live[t, which].astype(jnp.float32)
                 keep = jnp.full((block, width), keep, jnp.float32).astype(held.dtype)
                 view = held.at[z, pl.ds(at, block), pl.ds(t * width, width)]
                 view[...] = view[...] * keep
@@ -105,9 +97,24 @@
 
         lax.fori_loop(0, rows // block, one, 0, unroll=rows // block <= 8)
 
-    for c in range(CHUNKS):
-        load(c).wait()
-        mask(c)
+    live_load.wait()
+    load(0).wait()
+    mask(0)
+    pl.semaphore_wait(barrier, 1 + cores * ((z > 0).astype(jnp.int32) + (z < last).astype(jnp.int32)))
+
+    pan_in.wait()
+    code_in.wait()
+
+    @pl.when(is_end)
+    def _():
+        pan_help.start()
+        code_help.start()
+
+    def launch(c, _):
+        @pl.when(c > 0)
+        def _():
+            load(c).wait()
+            mask(c)
 
         @pl.when(goes_right)
         def _():
@@ -117,11 +124,14 @@
         def _():
             to_left(z, c).start()
 
-        if c == 0:
-            @pl.when(works)
-            def _():
-                pan_mate.start()
-                code_mate.start()
+        return 0
+
+    @pl.when(works)
+    def _():
+        pan_mate.start()
+        code_mate.start()
+
+    lax.fori_loop(0, CHUNKS, launch, 0)
 
     def build(g):
         copy = pltpu.make_async_copy(codes.at[g], codes_s.at[g], code_copy)
@@ -233,34 +243,43 @@
         code_pass.wait_recv()
         build(1)
 
-    @pl.when(works)
-    def _():
-        for c in range(CHUNKS):
-            if c + 1 < CHUNKS:
-                forward(c + 1)
-            settle(c)
-
-            @pl.when(helps)
-            def _():
-                multiply(1, c)
-                for core in range(cores):
-                    back_out(core, c).start()
-
-            multiply(0, c)
-            mate_out(c).start()
-            own_out(c).start()
+    def finish(c, _):
+        @pl.when(c + 1 < CHUNKS)
+        def _():
+            forward(c + 1)
+
+        settle(c)
+
+        @pl.when(helps)
+        def _():
+            multiply(1, c)
+            for core in range(cores):
+                back_out(core, c).start()
+
+        multiply(0, c)
+        mate_out(c).start()
+        own_out(c).start()
+        return 0
+
+    @pl.when(works)
+    def _():
+        lax.fori_loop(0, CHUNKS, finish, 0)
 
     @pl.when(is_end)
     def _():
         pan_help.wait_send()
         code_help.wait_send()
-        for c in range(CHUNKS):
+
+        def collect(c, _):
             for core in range(cores):
                 remote(
                     staged.at[0, 0, part(c)], out.at[spot(core, c)], mate_sem.at[c], out_recv.at[core, c], rep=mate
                 ).wait_recv()
-
-    for c in range(CHUNKS):
+            return 0
+
+        lax.fori_loop(0, CHUNKS, collect, 0)
+
+    def drain(c, _):
         @pl.when(goes_right)
         def _():
             to_right(z, c).wait_send()
@@ -269,11 +288,8 @@
         def _():
             to_left(z, c).wait_send()
 
-    @pl.when(works)
-    def _():
-        pan_mate.wait_send()
-        code_mate.wait_send()
-        for c in range(CHUNKS):
+        @pl.when(works)
+        def _():
             def one(d, _):
                 left, right = z - d, z + d
 
@@ -294,13 +310,24 @@
                 staged.at[0, 0, part(c)], out.at[spot(mate, c)], mate_sem.at[c], out_recv.at[mate, c], rep=mate
             ).wait_recv()
 
+        @pl.when(helps)
+        def _():
+            for core in range(cores):
+                back_out(core, c).wait_send()
+
+        return 0
+
+    lax.fori_loop(0, CHUNKS, drain, 0)
+
+    @pl.when(works)
+    def _():
+        pan_mate.wait_send()
+        code_mate.wait_send()
+
     @pl.when(helps)
     def _():
         pan_pass.wait_send()
         code_pass.wait_send()
-        for c in range(CHUNKS):
-            for core in range(cores):
-                back_out(core, c).wait_send()
 
 
 def per_device(amplitudes, live_mask, integrals, coupled_tiles):
@@ -314,19 +341,21 @@
         ladder_kernel,
         out_shape=jax.ShapeDtypeStruct((amplitudes.shape[0], width), kind),
         in_specs=[
-            pl.BlockSpec(memory_space=pl.ANY),
-            pl.BlockSpec(memory_space=pltpu.SMEM),
-            pl.BlockSpec(memory_space=pl.ANY),
-            pl.BlockSpec(memory_space=pl.ANY),
+            pl.BlockSpec(memory_space=pltpu.HBM),
+            pl.BlockSpec(memory_space=pltpu.HBM),
+            pl.BlockSpec(memory_space=pltpu.HBM),
+            pl.BlockSpec(memory_space=pltpu.HBM),
         ],
         out_specs=pl.BlockSpec(memory_space=pl.ANY),
         scratch_shapes=[
+            pltpu.SMEM(live_mask.shape[::-1], jnp.int32),
             pltpu.VMEM((count, half, tiles * width), kind),
             pltpu.VMEM((2, cores, tiles, ks, width, width), kind),
             pltpu.VMEM((2, cores, tiles, ks), jnp.int32),
             pltpu.SMEM((2, cores, tiles, ks), jnp.int32),
             pltpu.VMEM((2, count, tiles * width, tiles * width), kind),
             pltpu.VMEM((2, tiles, half, width), kind),
+            dma(()),
             dma((CHUNKS,)),
             dma((count, CHUNKS)),
             dma((count, CHUNKS)),
@@ -346,7 +375,7 @@
         compiler_params=pltpu.CompilerParams(
             collective_id=0, has_side_effects=True, vmem_limit_bytes=48 * 1024 * 1024
         ),
-    )(amplitudes, live_mask, integrals, coupled_tiles)
+    )(*[pltpu.with_memory_space_constraint(x, pltpu.HBM) for x in (amplitudes, live_mask.T, integrals, coupled_tiles)])
 
 
 def solution(mesh):

time: 26.7 us -> 23.3 us (0.87)
  local copies, waits for them, and re-layouts: 3.43 us -> 0.71 us
  Pallas kernels: 23.1 us -> 22.5 us
    unnamed x8 -> x1, local copies, waits for them, and re-layouts: 3.43 us -> 0.71 us
    pallas_call x1, Pallas kernels: 23.1 us -> 22.5 us  [per_device(): pl.pallas_call(ladder_kernel, out_shape=jax.ShapeDtypeStruct((amplitudes....]
where the time goes in v2:
time: 23.3 us; the launch traced here: 23.2 us
  Pallas kernels  22.5 us (97%)
  local copies, waits for them, and re-layouts  0.71 us (3%)
    pallas_call x1, Pallas kernels, per_device(): pl.pallas_call(ladder_kernel, out_shape=jax.ShapeDtypeStruct((amplitudes....  22.5 us
    unnamed x1, local copies, waits for them, and re-layouts  0.71 us

profile of v2, /device:TPU:0, one launch (start us, length us, event | category | flops | bytes accessed | tf_op | source)
XLA Modules:
  0.0 23.2 jit_solution(1970589049257287140)
XLA Ops:
  0.0 22.5 %shard_map.46 = bf16[1024,128]{1,0:T(8,128)(2,1)S(1)} custom-call(bf16[1024,256]{1,0:T(8,128)(2,1)} %amps.1, s32[2,32]{1,0:T(2,128)} %bitcast.1, bf16[2,2,128,128]{3,2,1,0:T(8,128)(2,1)} %ints.1, s32[2,2]{1,0:T(2,128)} %pattern.1), custom_call_target="tpu_custom_call" | custom-call | tf_op jit(solution)/shard_map/pallas_call | solution.py:340
  22.5 0.7 %copy.6 = bf16[1024,128]{1,0:T(8,128)(2,1)} copy(bf16[1024,128]{1,0:T(8,128)(2,1)S(1)} %shard_map.46) | data formatting | bytes 524288

commit v3 on v2

--- a/solution.py
+++ b/solution.py
@@ -109,6 +109,8 @@
     def _():
         pan_help.start()
         code_help.start()
+        pan_help.wait_send()
+        code_help.wait_send()
 
     def launch(c, _):
         @pl.when(c > 0)
@@ -155,7 +157,7 @@
     def arrive(j, c):
         to_right(j, c).wait_recv()
 
-    def forward(c):
+    def forward(c, _):
         def one(d, _):
             left, right = z - d, z + d
 
@@ -172,6 +174,7 @@
             return 0
 
         lax.fori_loop(1, count, one, 0)
+        return 0
 
     def settle(c):
         def one(d, _):
@@ -220,12 +223,6 @@
 
         lax.fori_loop(0, rows // step, one, 0)
 
-    @pl.when(works)
-    def _():
-        pan_mate.wait_recv()
-        code_mate.wait_recv()
-        build(0)
-
     @pl.when(helps)
     def _():
         pan_help.wait_recv()
@@ -235,7 +232,13 @@
 
     @pl.when(works)
     def _():
-        forward(0)
+        pan_mate.wait_recv()
+        code_mate.wait_recv()
+        build(0)
+
+    @pl.when(works)
+    def _():
+        lax.fori_loop(0, CHUNKS, forward, 0)
 
     @pl.when(helps)
     def _():
@@ -244,10 +247,6 @@
         build(1)
 
     def finish(c, _):
-        @pl.when(c + 1 < CHUNKS)
-        def _():
-            forward(c + 1)
-
         settle(c)
 
         @pl.when(helps)
@@ -267,9 +266,6 @@
 
     @pl.when(is_end)
     def _():
-        pan_help.wait_send()
-        code_help.wait_send()
-
         def collect(c, _):
             for core in range(cores):
                 remote(

time: 23.3 us -> 22.6 us (0.970)
  Pallas kernels: 22.5 us -> 21.7 us
    pallas_call x1, Pallas kernels: 22.5 us -> 21.7 us  [per_device(): pl.pallas_call(ladder_kernel, out_shape=jax.ShapeDtypeStruct((amplitudes....]
where the time goes in v3:
time: 22.6 us; the launch traced here: 22.4 us
  Pallas kernels  21.7 us (96%)
  local copies, waits for them, and re-layouts  0.71 us (3%)
    pallas_call x1, Pallas kernels, per_device(): pl.pallas_call(ladder_kernel, out_shape=jax.ShapeDtypeStruct((amplitudes....  21.7 us
    unnamed x1, local copies, waits for them, and re-layouts  0.71 us

profile of v3, /device:TPU:0, one launch (start us, length us, event | category | flops | bytes accessed | tf_op | source)
XLA Modules:
  0.0 22.4 jit_solution(7374698380597978118)
XLA Ops:
  0.0 21.7 %shard_map.46 = bf16[1024,128]{1,0:T(8,128)(2,1)S(1)} custom-call(bf16[1024,256]{1,0:T(8,128)(2,1)} %amps.1, s32[2,32]{1,0:T(2,128)} %bitcast.1, bf16[2,2,128,128]{3,2,1,0:T(8,128)(2,1)} %ints.1, s32[2,2]{1,0:T(2,128)} %pattern.1), custom_call_target="tpu_custom_call" | custom-call | tf_op jit(solution)/shard_map/pallas_call | solution.py:336
  21.7 0.7 %copy.6 = bf16[1024,128]{1,0:T(8,128)(2,1)} copy(bf16[1024,128]{1,0:T(8,128)(2,1)S(1)} %shard_map.46) | data formatting | bytes 524288
